TPU v7x, 32 devices: a whole 2x2x4 slice. The times are simulated.
32 devices in a mesh: row: 8 (over y, x, core), col: 4 (over z).
Axes of the slice: x: 2, y: 2, z: 4, core: 2. Of those that a mesh axis runs over, the one named last changes fastest.
Arguments:
- amplitudes: bfloat16 [64, 6400], P(('col', 'row')), may hold values from -6 to 6
- panel: bfloat16 [9600, 6400], P('col', 'row'), may hold values from -0.21875 to 0.21875
- irrep_ij: int32 [64], replicated, may hold values from 0 to 7
- irrep_ef: int32 [6400], replicated, may hold values from 0 to 7
Outputs:
- ladder: bfloat16 [64, 9600], P(('col', 'row'))
All inputs are finite; a program needn't handle non-finite values.
Results may differ from a plain program's by a relative error of at most 0.003.
Values may be sent and summed in bfloat16 or wider, within the bound.
A program may use at most 64 MiB of HBM per device.

v0:
```python
import jax
import jax.numpy as jnp
from jax import lax
from jax.sharding import PartitionSpec as P


def contract(left, right):
    return lax.dot_general(
        left, right, (((1,), (1,)), ((), ())), preferred_element_type=jnp.float32
    )


def ef_local(irrep_ij, irrep_ef, blocked):
    pair_rows = blocked.shape[0]
    pair_cols = blocked.shape[1]
    col_index = lax.axis_index("col")
    row_index = lax.axis_index("row")
    sym_rows = lax.dynamic_slice_in_dim(irrep_ij, col_index * pair_rows, pair_rows)
    sym_cols = lax.dynamic_slice_in_dim(irrep_ef, row_index * pair_cols, pair_cols)
    return jnp.where(sym_rows[:, None] == sym_cols[None, :], blocked, jnp.zeros_like(blocked))


def body(amplitudes, panel, irrep_ij, irrep_ef):
    blocked = lax.all_to_all(amplitudes, "row", split_axis=1, concat_axis=0, tiled=True)
    allowed = ef_local(irrep_ij, irrep_ef, blocked)
    partial_terms = contract(allowed, lax.all_gather(panel, "col", axis=0, tiled=True))
    summed = lax.psum_scatter(partial_terms, "row", scatter_dimension=0, tiled=True)
    return summed.astype(jnp.bfloat16)


def solution(mesh):
    in_specs = (P(("col", "row"), None), P("col", "row"), P(), P())
    out_specs = P(("col", "row"), None)
    return jax.shard_map(body, mesh=mesh, in_specs=in_specs, out_specs=out_specs, check_vma=False)
```

profile of v0, /device:TPU:0, one launch (start us, length us, event | category | flops | bytes accessed | tf_op | source)
XLA Modules:
  0.0 396.6 jit_solution(6917603864206018929)
XLA Ops:
  6.5 0.0 all-gather.3.cloned.1.call-start
  6.5 0.7 all-gather.3.cloned.1.call-update
  7.3 0.8 all_to_all.14
  8.1 0.6 copy.7
  8.7 5.2 %all-to-all-start = ((bf16[2,8,800]{2,0,1:T(2,128)(2,1)}), bf16[2,8,800]{2,0,1:T(2,128)(2,1)S(1)}, u32[]{:S(2)}, u32[]{:S(2)}) async-start(bf16[2,8,800]{2,0,1:T(2,128)(2,1)} %copy.7), calls=%async_computation | async-start | bytes 57344 | tf_op jit(solution)/shard_map/all_to_all | solution.py:24
  13.9 0.8 dynamic_slice.7
  14.7 0.7 dynamic_slice.6
  15.4 1.2 dynamic-slice
  17.2 1.5 all-to-all-done
  18.8 259.8 %all-gather.3.cloned.1.call-done = bf16[4,2400,800]{1,2,0:T(8,128)(2,1)} async-done(((bf16[1,2400,800]{1,2,0:T(8,128)(2,1)}), bf16[4,2400,800]{1,2,0:T(8,128)(2,1)}) %all-gather.3.cloned.1.call-update) | async-done | bytes 15360016 | tf_op jit(solution)/shard_map/all_gather | solution.py:26
  278.6 48.0 %copy.8 = bf16[4,2400,800]{1,0,2:T(4,128)(2,1)} copy(bf16[4,2400,800]{1,2,0:T(8,128)(2,1)} %all-gather.3.cloned.1.call-done) | data formatting | bytes 30720000 | tf_op jit(solution)/shard_map/all_gather | solution.py:26
  326.6 24.8 %reshape.6 = bf16[9600,800]{0,1:T(8,128)(2,1)} reshape(bf16[4,2400,800]{1,0,2:T(4,128)(2,1)} %copy.8) | data formatting | bytes 30720000
  351.5 6.6 %fusion = f32[16,9600]{1,0:T(8,128)S(1)} fusion(bf16[9600,800]{0,1:T(8,128)(2,1)} %reshape.6, bf16[16,800]{1,0:T(8,128)(2,1)S(1)} %all_to_all.17, s32[800]{0:T(1024)S(1)} %dynamic_slice.7, s32[16]{0:T(128)S(1)} %dynamic_slice.6), kind=kOutput, calls=%fused_computation.2 | convolution fusion | flops 245785600 | bytes 16003264 | tf_op jit(solution)/shard_map/dot_general | solution.py:8
  358.1 31.0 %all-reduce.2 = bf16[16,9600]{1,0:T(8,128)(2,1)S(1)} all-reduce(f32[16,9600]{1,0:T(8,128)S(1)} %fusion), channel_id=2, replica_groups=mesh['row'=8,'col'=4] {'row'}, use_global_device_ids=true, to_apply=%region_0.1.clone | all-reduce | flops 153600 | bytes 921600
  389.1 0.7 dynamic-slice_convert_fusion
  (1 shorter events, 0.0 us)
Async XLA Ops:
  6.5 272.1 %all-gather.3.cloned.1.call-start = ((), (), s32[]{:S(2)}) async-start(), calls=%async_computation.1 | async-start | bytes 19456000 | tf_op jit(solution)/shard_map/all_gather | solution.py:26
  8.7 10.0 %all-to-all-start = ((bf16[2,8,800]{2,0,1:T(2,128)(2,1)}), bf16[2,8,800]{2,0,1:T(2,128)(2,1)S(1)}, u32[]{:S(2)}, u32[]{:S(2)}) async-start(bf16[2,8,800]{2,0,1:T(2,128)(2,1)} %copy.7), calls=%async_computation | async-start | bytes 57344 | tf_op jit(solution)/shard_map/all_to_all | solution.py:24
Sparse Core Ops, SparseCore 0:
  8.9 269.6 all-gather.2
where the time goes:
time: 398 us; the launch traced here: 397 us
  waiting for transfers between devices  262 us (66%)
  local copies, waits for them, and re-layouts  77.8 us (20%)
  blocking collectives  31 us (8%)
  between operations  14 us (4%)
  matrix products  6.61 us (2%)
  starting transfers between devices  5.17 us (1%)
    all_gather x1, waiting for transfers between devices, body(): lax.all_gather(panel, 'col', axis=0, tiled=True)  260 us
    all_gather x1, local copies, waits for them, and re-layouts, body(): lax.all_gather(panel, 'col', axis=0, tiled=True)  48 us
    unnamed x1, blocking collectives  31 us
    unnamed x2, local copies, waits for them, and re-layouts  26.1 us
  transfers between devices with their start and end apart: 2, of which 2 were waited for; matrix products, arithmetic and copies ran while one was open for 1% of the time, Pallas kernels for 0%

commit v1 on v0

--- a/solution.py
+++ b/solution.py
@@ -2,6 +2,28 @@
 import jax.numpy as jnp
 from jax import lax
 from jax.sharding import PartitionSpec as P
+
+
+def in_order(blocks, dim):
+    dims = list(blocks.shape[1:])
+    dims[dim] *= blocks.shape[0]
+    return jnp.moveaxis(blocks, 0, dim).reshape(dims)
+
+
+def collect(array, axis, dim):
+    length = lax.axis_size(axis)
+    pairs = [(i, (i + 1) % length) for i in range(length)]
+    back = [(b, a) for a, b in pairs]
+    lower, upper = ([], [])
+    for step in range(length - 1):
+        if step % 2 == 0:
+            lower.append(lax.ppermute(lower[-1] if lower else array, axis, pairs))
+        else:
+            upper.append(lax.ppermute(upper[-1] if upper else array, axis, back))
+    tiles = jnp.stack([*lower[::-1], array, *upper])
+    shift = lax.axis_index(axis) - len(lower)
+    tiles = tiles[(jnp.arange(length) - shift) % length]
+    return in_order(tiles, dim)
 
 
 def contract(left, right):
@@ -23,7 +45,7 @@
 def body(amplitudes, panel, irrep_ij, irrep_ef):
     blocked = lax.all_to_all(amplitudes, "row", split_axis=1, concat_axis=0, tiled=True)
     allowed = ef_local(irrep_ij, irrep_ef, blocked)
-    partial_terms = contract(allowed, lax.all_gather(panel, "col", axis=0, tiled=True))
+    partial_terms = contract(allowed, collect(panel, "col", 0))
     summed = lax.psum_scatter(partial_terms, "row", scatter_dimension=0, tiled=True)
     return summed.astype(jnp.bfloat16)
 

time: 398 us -> 397 us (level)
  other arithmetic: 0 us -> 38.7 us
  waiting for transfers between devices: 262 us -> 242 us
  between operations: 14 us -> 0.68 us
  local copies, waits for them, and re-layouts: 77.8 us -> 67.8 us
    all_gather x1 -> x0, waiting for transfers between devices: 260 us -> none  [body(): lax.all_gather(panel, 'col', axis=0, tiled=True)]
    ppermute x0 -> x3, waiting for transfers between devices: none -> 241 us  [the longest x2 169 us: collect(): lower.append(lax.ppermute(lower[-1] if lower else array, axis, pairs))]
    gather x0 -> x19, local copies, waits for them, and re-layouts: none -> 62.7 us
    all_gather x1 -> x0, local copies, waits for them, and re-layouts: 48 us -> none  [body(): lax.all_gather(panel, 'col', axis=0, tiled=True)]
    unnamed x2 -> x3, local copies, waits for them, and re-layouts: 26.1 us -> 1.27 us
    unnamed x0 -> x2, other arithmetic: none -> 19 us
    another operation x0 -> x1, other arithmetic: none -> 12.9 us  [collect(): tiles = jnp.stack([*lower[::-1], array, *upper])]
    gather x0 -> x2, other arithmetic: none -> 6.72 us  [collect(): tiles = tiles[(jnp.arange(length) - shift) % length]]
  transfers between devices with their start and end apart: 2 -> 4, of which waited for: 2 -> 4; matrix products, arithmetic and copies ran while one was open for 1% -> 1% of each run, Pallas kernels for 0% -> 0%
where the time goes in v1:
time: 397 us; the launch traced here: 395 us
  waiting for transfers between devices  242 us (61%)
  local copies, waits for them, and re-layouts  67.8 us (17%)
  other arithmetic  38.7 us (10%)
  blocking collectives  28.9 us (7%)
  starting transfers between devices  9.02 us (2%)
  matrix products  8.26 us (2%)
    ppermute x2, waiting for transfers between devices, collect(): lower.append(lax.ppermute(lower[-1] if lower else array, axis, pairs))  169 us
    ppermute x1, waiting for transfers between devices, collect(): upper.append(lax.ppermute(upper[-1] if upper else array, axis, back))  71.7 us
    gather x16, local copies, waits for them, and re-layouts  37.1 us
    unnamed x1, blocking collectives  28.9 us
    gather x3, local copies, waits for them, and re-layouts, collect(): tiles = tiles[(jnp.arange(length) - shift) % length]  25.6 us
    unnamed x2, other arithmetic  19 us
    another operation x1, other arithmetic, collect(): tiles = jnp.stack([*lower[::-1], array, *upper])  12.9 us
    dot_general x1, matrix products, contract(): lax.dot_general(left, right, (((1,), (1,)), ((), ())), preferred_element_...  8.26 us
  transfers between devices with their start and end apart: 4, of which 4 were waited for; matrix products, arithmetic and copies ran while one was open for 1% of the time, Pallas kernels for 0%

profile of v1, /device:TPU:0, one launch (start us, length us, event | category | flops | bytes accessed | tf_op | source)
XLA Modules:
  0.0 395.4 jit_solution(14728387603039528476)
XLA Ops:
  0.0 3.0 collective-permute-start
  3.0 2.0 collective-permute-start.2
  5.1 85.3 %collective-permute-done = bf16[2400,800]{0,1:T(8,128)(2,1)} collective-permute-done((bf16[2400,800]{0,1:T(8,128)(2,1)}, bf16[2400,800]{0,1:T(8,128)(2,1)}, u32[]{:S(2)}, u32[]{:S(2)}) %collective-permute-start) | collective-permute-done | bytes 3840032 | tf_op jit(solution)/shard_map/ppermute | solution.py:20
  90.3 0.0 collective-permute-start.1
  90.3 0.8 all_to_all.12
  91.2 0.6 copy.13
  91.8 4.0 %all-to-all-start = ((bf16[2,8,800]{2,0,1:T(2,128)(2,1)}), bf16[2,8,800]{2,0,1:T(2,128)(2,1)S(1)}, u32[]{:S(2)}, u32[]{:S(2)}) async-start(bf16[2,8,800]{2,0,1:T(2,128)(2,1)} %copy.13), calls=%async_computation | async-start | bytes 57344 | tf_op jit(solution)/shard_map/all_to_all | solution.py:46
  95.8 0.7 dynamic_slice.6
  96.6 0.1 eq.18
  96.7 0.8 dynamic_slice.7
  97.4 1.3 dynamic-slice.4
  99.3 1.3 all-to-all-done
  100.6 0.1 compare_select_fusion
  100.7 71.7 %collective-permute-done.2 = bf16[2400,800]{0,1:T(8,128)(2,1)} collective-permute-done((bf16[2400,800]{0,1:T(8,128)(2,1)}, bf16[2400,800]{0,1:T(8,128)(2,1)}, u32[]{:S(2)}, u32[]{:S(2)}) %collective-permute-start.2) | collective-permute-done | bytes 3840032 | tf_op jit(solution)/shard_map/ppermute | solution.py:22
  172.5 83.8 %collective-permute-done.1 = bf16[2400,800]{0,1:T(8,128)(2,1)} collective-permute-done((bf16[2400,800]{0,1:T(8,128)(2,1)}, bf16[2400,800]{0,1:T(8,128)(2,1)}, u32[]{:S(2)}, u32[]{:S(2)}) %collective-permute-start.1) | collective-permute-done | bytes 3840032 | tf_op jit(solution)/shard_map/ppermute | solution.py:20
  256.3 0.0 copy-start
  256.3 6.7 %pad_maximum_fusion.2 = bf16[4,1120,800]{1,2,0:T(8,128)(2,1)} fusion(bf16[1,2400,800]{1,2,0:T(8,128)(2,1)} %bitcast.4, bf16[1,2400,800]{1,2,0:T(8,128)(2,1)} %bitcast.16, bf16[1,2400,800]{1,2,0:T(8,128)(2,1)} %bitcast.2, bf16[1,2400,800]{1,2,0:T(8,128)(2,1)} %bitcast.1), kind=kLoop, calls=%fused_computation.6 | loop fusion | flops 28672000 | bytes 22528000 | tf_op jit(solution)/shard_map/gather | solution.py:25
  263.0 0.0 copy-done
  263.0 12.9 %pad_maximum_fusion.1 = bf16[4,2400,800]{1,2,0:T(8,128)(2,1)} fusion(bf16[1,2400,800]{1,2,0:T(8,128)(2,1)} %bitcast.4, bf16[1,2400,800]{1,2,0:T(8,128)(2,1)S(1)} %bitcast.17, bf16[1,2400,800]{1,2,0:T(8,128)(2,1)} %bitcast.2, bf16[1,2400,800]{1,2,0:T(8,128)(2,1)} %bitcast.1), kind=kLoop, calls=%fused_computation.5 | loop fusion | flops 23040000 | bytes 30720000 | tf_op jit(solution)/shard_map/stack | solution.py:23
  275.9 7.4 %gather_fusion = bf16[4,1120,800]{1,2,0:T(8,128)(2,1)} fusion(bf16[4,1120,800]{1,2,0:T(8,128)(2,1)} %pad_maximum_fusion.2, s32[1024]{0:T(1024)S(1)} %pad_clamp_fusion), kind=kCustom, calls=%fused_computation | custom fusion | bytes 14336016 | tf_op jit(solution)/shard_map/gather | solution.py:25
  283.3 11.2 %copy.15 = bf16[4,1120,800]{2,1,0:T(8,128)(2,1)} copy(bf16[4,1120,800]{1,2,0:T(8,128)(2,1)} %gather_fusion) | data formatting | bytes 14336000 | tf_op jit(solution)/shard_map/gather | solution.py:25
  294.4 7.0 %mini-gather-slice.2 = bf16[4,1280,800]{1,2,0:T(8,128)(2,1)} slice(bf16[4,2400,800]{1,2,0:T(8,128)(2,1)} %pad_maximum_fusion.1), slice={[0:4], [0:1280], [0:800]} | slice | bytes 16384000 | tf_op jit(solution)/shard_map/gather | solution.py:25
  301.5 37.2 %while.1 = (s32[]{:T(128)}, bf16[4,1280,800]{1,2,0:T(8,128)(2,1)}, s32[4,1]{0,1:T(1,128)S(1)}, bf16[4,1280,800]{2,1,0:T(8,128)(2,1)}, s32[]{:T(128)}) while((s32[]{:T(128)}, bf16[4,1280,800]{1,2,0:T(8,128)(2,1)}, s32[4,1]{0,1:T(1,128)S(1)}, bf16[4,1280,800]{2,1,0:T(8,128)(2,1)}, s32[]{:T(128)}) %tuple.17), condition=%wide.while_cond, body=%wide.while_body.sunk | while | flops 2 | bytes 12533849 | solution.py:25
  301.5 0.6 constant_dynamic-slice_fusion.4
  302.0 3.7 constant_dynamic-slice_fusion.5
  305.7 3.4 copy.18
  309.1 1.6 constant_dynamic-update-slice_fusion.2
  310.7 0.6 constant_dynamic-slice_fusion.4
  311.3 3.7 constant_dynamic-slice_fusion.5
  315.0 3.4 copy.18
  318.4 1.6 constant_dynamic-update-slice_fusion.2
  320.0 0.6 constant_dynamic-slice_fusion.4
  320.5 3.7 constant_dynamic-slice_fusion.5
  324.2 3.4 copy.18
  327.7 1.6 constant_dynamic-update-slice_fusion.2
  329.3 0.6 constant_dynamic-slice_fusion.4
  329.9 3.7 constant_dynamic-slice_fusion.5
  333.6 3.4 copy.18
  337.0 1.6 constant_dynamic-update-slice_fusion.2
  338.6 19.0 %pad_maximum_fusion = bf16[4,2400,800]{2,1,0:T(8,128)(2,1)} fusion(bf16[4,1120,800]{2,1,0:T(8,128)(2,1)} %copy.15, bf16[4,1280,800]{2,1,0:T(8,128)(2,1)} %get-tuple-element.12), kind=kLoop, calls=%fused_computation.4 | loop fusion | flops 30720000 | bytes 30720000
  357.6 8.3 %fusion.2 = f32[16,9600]{1,0:T(8,128)S(1)} fusion(bf16[16,800]{1,0:T(8,128)(2,1)S(1)} %select_n.40, bf16[9600,800]{1,0:T(8,128)(2,1)} %bitcast.15), kind=kOutput, calls=%fused_computation.16 | convolution fusion | flops 245760000 | bytes 16000000 | tf_op jit(solution)/shard_map/dot_general | solution.py:30
  365.8 28.9 %all-reduce.2 = bf16[16,9600]{1,0:T(8,128)(2,1)S(1)} all-reduce(f32[16,9600]{1,0:T(8,128)S(1)} %fusion.2), channel_id=2, replica_groups=mesh['row'=8,'col'=4] {'row'}, use_global_device_ids=true, to_apply=%region_0.1.clone | all-reduce | flops 153600 | bytes 921600
  394.7 0.7 dynamic-slice_convert_fusion
  (5 shorter events, 0.1 us)
Async XLA Ops:
  0.0 90.3 %collective-permute-start = (bf16[2400,800]{0,1:T(8,128)(2,1)}, bf16[2400,800]{0,1:T(8,128)(2,1)}, u32[]{:S(2)}, u32[]{:S(2)}) collective-permute-start(bf16[2400,800]{0,1:T(8,128)(2,1)} %param.5), channel_id=1, source_target_pairs={{0,1},{1,2},{2,3},{3,0},{4,5},{5,6},{6,7},{7,4},{8,9},{9,10},{10,1... | collective-permute-start | bytes 11520008 | tf_op jit(solution)/shard_map/ppermute | solution.py:20
  3.0 169.5 %collective-permute-start.2 = (bf16[2400,800]{0,1:T(8,128)(2,1)}, bf16[2400,800]{0,1:T(8,128)(2,1)}, u32[]{:S(2)}, u32[]{:S(2)}) collective-permute-start(bf16[2400,800]{0,1:T(8,128)(2,1)} %param.5), channel_id=1, source_target_pairs={{1,0},{2,1},{3,2},{0,3},{5,4},{6,5},{7,6},{4,7},{9,8},{10,9},{11,1... | collective-permute-start | bytes 11520008 | tf_op jit(solution)/shard_map/ppermute | solution.py:22
  90.3 165.9 %collective-permute-start.1 = (bf16[2400,800]{0,1:T(8,128)(2,1)}, bf16[2400,800]{0,1:T(8,128)(2,1)}, u32[]{:S(2)}, u32[]{:S(2)}) collective-permute-start(bf16[2400,800]{0,1:T(8,128)(2,1)} %collective-permute-done), channel_id=1, source_target_pairs={{0,1},{1,2},{2,3},{3,0},{4,5},{5,6},{6,7},{7,4},{8,9},{9,10},{10,1... | collective-permute-start | bytes 11520008 | tf_op jit(solution)/shard_map/ppermute | solution.py:20
  91.8 8.8 %all-to-all-start = ((bf16[2,8,800]{2,0,1:T(2,128)(2,1)}), bf16[2,8,800]{2,0,1:T(2,128)(2,1)S(1)}, u32[]{:S(2)}, u32[]{:S(2)}) async-start(bf16[2,8,800]{2,0,1:T(2,128)(2,1)} %copy.13), calls=%async_computation | async-start | bytes 57344 | tf_op jit(solution)/shard_map/all_to_all | solution.py:46
  256.3 6.7 %copy-start = (bf16[2400,800]{0,1:T(8,128)(2,1)S(1)}, bf16[2400,800]{0,1:T(8,128)(2,1)}, u32[]{:S(2)}) copy-start(bf16[2400,800]{0,1:T(8,128)(2,1)} %param.5) | copy-start | bytes 11520004

commit v2 on v0

--- a/solution.py
+++ b/solution.py
@@ -2,6 +2,18 @@
 import jax.numpy as jnp
 from jax import lax
 from jax.sharding import PartitionSpec as P
+
+
+def exchange_directly(value, axis, split, join):
+    ways, here = (lax.axis_size(axis), lax.axis_index(axis))
+    width = value.shape[split] // ways
+    turned = jnp.roll(value, -here * width, axis=split)
+    got = [lax.slice_in_dim(turned, 0, width, axis=split)]
+    for far in range(1, ways):
+        sent = lax.slice_in_dim(turned, far * width, (far + 1) * width, axis=split)
+        got.append(lax.ppermute(sent, axis, [(d, (d + far) % ways) for d in range(ways)]))
+    line = jnp.concatenate(got[::-1], axis=join)
+    return jnp.roll(line, (here + 1) * got[0].shape[join], axis=join)
 
 
 def contract(left, right):
@@ -21,7 +33,7 @@
 
 
 def body(amplitudes, panel, irrep_ij, irrep_ef):
-    blocked = lax.all_to_all(amplitudes, "row", split_axis=1, concat_axis=0, tiled=True)
+    blocked = exchange_directly(amplitudes, "row", 1, 0)
     allowed = ef_local(irrep_ij, irrep_ef, blocked)
     partial_terms = contract(allowed, lax.all_gather(panel, "col", axis=0, tiled=True))
     summed = lax.psum_scatter(partial_terms, "row", scatter_dimension=0, tiled=True)

time: 398 us -> 397 us (level)
    ppermute x0 -> x7, starting transfers between devices: none -> 8.32 us  [exchange_directly(): lax.ppermute(sent, axis, [(d, (d + far) % ways) for d in range(ways)])]
    all_to_all x1 -> x0, starting transfers between devices: 5.17 us -> none  [body(): lax.all_to_all(amplitudes, 'row', split_axis=1, concat_axis=0, tiled=True)]
  transfers between devices with their start and end apart: 2 -> 8, of which waited for: 2 -> 2; matrix products, arithmetic and copies ran while one was open for 1% -> 1% of each run, Pallas kernels for 0% -> 0%
where the time goes in v2:
time: 397 us
  waiting for transfers between devices  259 us (65%)
  local copies, waits for them, and re-layouts  76.5 us (19%)
  blocking collectives  31 us (8%)
  between operations  14.1 us (4%)
  starting transfers between devices  8.32 us (2%)
  matrix products  6.61 us (2%)
    all_gather x1, waiting for transfers between devices, body(): lax.all_gather(panel, 'col', axis=0, tiled=True)  258 us
    all_gather x1, local copies, waits for them, and re-layouts, body(): lax.all_gather(panel, 'col', axis=0, tiled=True)  48 us
    unnamed x1, blocking collectives  31 us
    unnamed x2, local copies, waits for them, and re-layouts  26.1 us
    ppermute x7, starting transfers between devices, exchange_directly(): lax.ppermute(sent, axis, [(d, (d + far) % ways) for d in range(ways)])  8.32 us
  transfers between devices with their start and end apart: 8, of which 2 were waited for; matrix products, arithmetic and copies ran while one was open for 1% of the time, Pallas kernels for 0%

profile of v2, /device:TPU:0, one launch (start us, length us, event | category | flops | bytes accessed | tf_op | source)
XLA Modules:
  0.0 396.6 jit_solution(7442310885666154230)
XLA Ops:
  6.5 0.0 all-gather.3.cloned.1.call-start
  6.5 0.7 all-gather.3.cloned.1.call-update
  7.3 0.9 fusion.4
  8.2 0.1 fusion.8
  8.3 3.4 collective-permute-start
  11.7 0.6 collective-permute-start.1
  12.4 0.2 collective-permute-start.2
  12.6 1.6 collective-permute-start.3
  14.2 0.1 collective-permute-start.4
  14.3 0.0 collective-permute-done
  14.3 2.3 collective-permute-start.5
  16.6 0.0 collective-permute-done.1
  16.6 0.0 collective-permute-start.6
  16.6 0.8 dynamic_slice.15
  17.4 0.7 dynamic_slice.14
  18.1 1.2 dynamic-slice
  20.0 0.0 collective-permute-done.2
  20.1 0.0 collective-permute-done.3
  20.1 0.0 collective-permute-done.4
  20.1 0.0 collective-permute-done.5
  20.1 0.5 collective-permute-done.6
  20.6 0.1 concatenate.11
  20.7 257.9 %all-gather.3.cloned.1.call-done = bf16[4,2400,800]{1,2,0:T(8,128)(2,1)} async-done(((bf16[1,2400,800]{1,2,0:T(8,128)(2,1)}), bf16[4,2400,800]{1,2,0:T(8,128)(2,1)}) %all-gather.3.cloned.1.call-update) | async-done | bytes 15360016 | tf_op jit(solution)/shard_map/all_gather | solution.py:38
  278.6 48.0 %copy.6 = bf16[4,2400,800]{1,0,2:T(4,128)(2,1)} copy(bf16[4,2400,800]{1,2,0:T(8,128)(2,1)} %all-gather.3.cloned.1.call-done) | data formatting | bytes 30720000 | tf_op jit(solution)/shard_map/all_gather | solution.py:38
  326.6 24.8 %reshape.3 = bf16[9600,800]{0,1:T(8,128)(2,1)} reshape(bf16[4,2400,800]{1,0,2:T(4,128)(2,1)} %copy.6) | data formatting | bytes 30720000
  351.5 6.6 %fusion = f32[16,9600]{1,0:T(8,128)S(1)} fusion(bf16[9600,800]{0,1:T(8,128)(2,1)} %reshape.3, bf16[32,800]{1,0:T(8,128)(2,1)S(1)} %concatenate.11, s32[]{:T(128)S(6)} %select_n.38, s32[800]{0:T(1024)S(1)} %dynamic_slice.15, s32[16]{0:T(128)S(1)} %dynamic_slice.14), kind=kOutput, calls=%fused_computation.4 | convolution fusion | flops 245785600 | bytes 16007684 | tf_op jit(solution)/shard_map/dot_general | solution.py:20
  358.1 31.0 %all-reduce.2 = bf16[16,9600]{1,0:T(8,128)(2,1)S(1)} all-reduce(f32[16,9600]{1,0:T(8,128)S(1)} %fusion), channel_id=2, replica_groups=mesh['row'=8,'col'=4] {'row'}, use_global_device_ids=true, to_apply=%region_0.1.clone | all-reduce | flops 153600 | bytes 921600
  389.1 0.7 dynamic-slice_convert_fusion
Async XLA Ops:
  6.5 272.1 %all-gather.3.cloned.1.call-start = ((), (), s32[]{:S(2)}) async-start(), calls=%async_computation | async-start | bytes 19456000 | tf_op jit(solution)/shard_map/all_gather | solution.py:38
  8.3 6.0 %collective-permute-start = (bf16[2,800]{1,0:T(2,128)(2,1)S(1)}, bf16[2,800]{1,0:T(2,128)(2,1)S(1)}, u32[]{:S(2)}, u32[]{:S(2)}) collective-permute-start(bf16[2,800]{1,0:T(2,128)(2,1)S(1)} %get-tuple-element.12), channel_id=1, source_target_pairs={{0,28},{4,0},{8,4},{12,8},{16,12},{20,16},{24,20},{28,24},{1,29},{... | collective-permute-start | bytes 9608 | tf_op jit(solution)/shard_map/ppermute | solution.py:14
  11.7 4.9 %collective-permute-start.1 = (bf16[2,800]{1,0:T(2,128)(2,1)S(1)}, bf16[2,800]{1,0:T(2,128)(2,1)S(1)}, u32[]{:S(2)}, u32[]{:S(2)}) collective-permute-start(bf16[2,800]{1,0:T(2,128)(2,1)S(1)} %get-tuple-element.11), channel_id=1, source_target_pairs={{0,24},{4,28},{8,0},{12,4},{16,8},{20,12},{24,16},{28,20},{1,25},{... | collective-permute-start | bytes 9608 | tf_op jit(solution)/shard_map/ppermute | solution.py:14
  12.4 7.7 %collective-permute-start.2 = (bf16[2,800]{1,0:T(2,128)(2,1)S(1)}, bf16[2,800]{1,0:T(2,128)(2,1)S(1)}, u32[]{:S(2)}, u32[]{:S(2)}) collective-permute-start(bf16[2,800]{1,0:T(2,128)(2,1)S(1)} %get-tuple-element.10), channel_id=1, source_target_pairs={{0,20},{4,24},{8,28},{12,0},{16,4},{20,8},{24,12},{28,16},{1,21},{... | collective-permute-start | bytes 9608 | tf_op jit(solution)/shard_map/ppermute | solution.py:14
  12.6 7.4 %collective-permute-start.3 = (bf16[2,800]{1,0:T(2,128)(2,1)S(1)}, bf16[2,800]{1,0:T(2,128)(2,1)S(1)}, u32[]{:S(2)}, u32[]{:S(2)}) collective-permute-start(bf16[2,800]{1,0:T(2,128)(2,1)S(1)} %get-tuple-element.9), channel_id=1, source_target_pairs={{0,16},{4,20},{8,24},{12,28},{16,0},{20,4},{24,8},{28,12},{1,17},{... | collective-permute-start | bytes 9608 | tf_op jit(solution)/shard_map/ppermute | solution.py:14
  14.2 5.9 %collective-permute-start.4 = (bf16[2,800]{1,0:T(2,128)(2,1)S(1)}, bf16[2,800]{1,0:T(2,128)(2,1)S(1)}, u32[]{:S(2)}, u32[]{:S(2)}) collective-permute-start(bf16[2,800]{1,0:T(2,128)(2,1)S(1)} %get-tuple-element.8), channel_id=1, source_target_pairs={{0,12},{4,16},{8,20},{12,24},{16,28},{20,0},{24,4},{28,8},{1,13},{... | collective-permute-start | bytes 9608 | tf_op jit(solution)/shard_map/ppermute | solution.py:14
  14.3 5.8 %collective-permute-start.5 = (bf16[2,800]{1,0:T(2,128)(2,1)S(1)}, bf16[2,800]{1,0:T(2,128)(2,1)S(1)}, u32[]{:S(2)}, u32[]{:S(2)}) collective-permute-start(bf16[2,800]{1,0:T(2,128)(2,1)S(1)} %get-tuple-element.7), channel_id=1, source_target_pairs={{0,8},{4,12},{8,16},{12,20},{16,24},{20,28},{24,0},{28,4},{1,9},{5... | collective-permute-start | bytes 9608 | tf_op jit(solution)/shard_map/ppermute | solution.py:14
  16.6 3.9 collective-permute-start.6
Sparse Core Ops, SparseCore 0:
  8.9 269.6 all-gather.2
